TPU v7x, 128 devices: a whole 4x4x4 slice. The times are simulated.
128 devices in a mesh: lat: 8 (over x, core), lon: 16 (over y, z).
Axes of the slice: x: 4, y: 4, z: 4, core: 2. Of those that a mesh axis runs over, the one named last changes fastest.
Arguments:
- tracers: float32 [10, 6, 128, 4096], P(None, None, 'lat', 'lon'), may hold values from 0.05 to 4
- forcing_groups: float32 [128, 128, 1728], P(('lat', 'lon')), as said below
- group_tiles: int32 [128, 128], P(('lat', 'lon')), may hold values from 0 to 127, each once within a row
- ocean_mask: int32 [128, 4096], P('lat', 'lon'), may hold values 0 or 1
- bio_rates: float32 [10, 10], replicated, may hold values from -2 to 2
- agent_traits: float32 [8, 16, 16, 64, 128], P('lat', 'lon'), may hold values from -6 to 6
- agent_cells: int32 [8, 16, 16, 128], P('lat'), may hold values from 0 to 4095
- agent_counts: int32 [8, 16, 16], P('lat'), may hold values from 0 to 128, as said below
- trait_weights: float32 [64, 64], replicated, may hold values from -0.75 to 0.75
- env_weights: float32 [60, 64], replicated, may hold values from -0.75 to 0.75
Outputs:
- tracers_out: float32 [10, 6, 128, 4096], P(None, None, 'lat', 'lon')
- agent_state: float32 [8, 16, 16, 64, 128], P('lat', 'lon')
Inputs may be any that keep to these rules, and one draw needn't show every extreme that they name: `group_tiles`: each row lists every tile exactly once. `agent_counts`: live slots come first in each block; in every draw, all blocks bound for some one tile are full. `forcing_groups`: fields u and v lie in -0.2 to 0.2, kappa in 0.01 to 0.12.
All inputs are finite; a program needn't handle non-finite values. No bound on the sum of `ocean_mask` on one device may be relied on, other than what follows from the above.
Results may differ from a plain program's by a relative error of at most 0.0001.
Values sent between devices are 32-bit elements; how exact they have to be, the bound alone decides.
No kernel may reach another device: no remote copies, remote signals or barrier semaphores. Data moves between devices by JAX's collectives and lax.ppermute only.
A program may use at most 64 MiB of HBM per device.

v0:
```python
import jax
import jax.numpy as jnp
from jax import lax
from jax.experimental import pallas as pl
from jax.experimental.pallas import tpu as pltpu
from jax.sharding import PartitionSpec as P

NTR = 10
LEV = 6
SUBS = 3
CY = 16
CX = 256
BIO_STEP = 0.2

F32 = jnp.float32
BF16 = jnp.bfloat16

LINES = 14
BUSY = 10**12
FR = 26
NF = NTR * LEV + 1


def call(kernel, outs, scratch=(), limit=8, flops=0, in_specs=None, out_specs=None):
    return pl.pallas_call(
        kernel,
        out_shape=outs,
        scratch_shapes=list(scratch),
        **({"in_specs": in_specs} if in_specs else {}),
        **({"out_specs": out_specs} if out_specs else {}),
        compiler_params=pltpu.CompilerParams(vmem_limit_bytes=limit * 1024 * 1024),
        cost_estimate=pl.CostEstimate(flops=flops, bytes_accessed=0, transcendentals=0),
    )


def full(*shape, dtype=F32):
    return jax.ShapeDtypeStruct(shape, dtype)


def three_parts(x):
    hi = x.astype(BF16)
    rest = x - hi.astype(F32)
    mid = rest.astype(BF16)
    lo = (rest - mid.astype(F32)).astype(BF16)
    return hi, mid, lo


def dot(a, b):
    return jnp.dot(a, b, preferred_element_type=F32)


def lane_iota(rows=8):
    return lax.broadcasted_iota(jnp.int32, (rows, 128), 1)


def sort_bands_kernel(bands_ref, tiles_ref, out_ref, xs_ref):
    reader = lax.axis_index("lat") * 16 + lax.axis_index("lon")
    case = lax.rem(reader, 4)
    rows = 16
    for i in range(4):

        @pl.when(case == i)
        def _(i=i):
            spare = 0 if i % 2 else 64
            first = (0, 1, 1, 2)[i]
            lane = lane_iota(rows)
            pad = jnp.zeros((rows, 64), F32)
            for g in range(128 // rows):
                here = pl.ds(g * rows, rows)
                x = bands_ref[0, here, :]
                x = jnp.concatenate([pad, x] if i % 2 else [x, pad], axis=1)
                xs_ref[here, : LINES * 128] = x
                ends = jnp.zeros((rows, 128), F32)
                starts = jnp.zeros((rows, 128), F32)
                for j in range(7):
                    line = first + 2 * j
                    at = spare + 8 * j
                    if not (i == 3 and j == 6):
                        moved = x[:, line * 128 : line * 128 + 128]
                        if at:
                            moved = pltpu.roll(moved, at, 1)
                        starts = jnp.where((lane >= at) & (lane < at + 3), moved, starts)
                    if not (i == 0 and j == 0):
                        moved = x[:, line * 128 - 128 : line * 128]
                        if (at + 8) % 128:
                            moved = pltpu.roll(moved, at + 8, 1)
                        ends = jnp.where((lane >= at + 5) & (lane < at + 8), moved, ends)
                xs_ref[here, LINES * 128 : LINES * 128 + 128] = ends
                xs_ref[here, LINES * 128 + 128 :] = starts

    tiles = tiles_ref[0:1, :]
    me = lax.broadcasted_iota(jnp.int32, (128, 128), 0)
    west = (me & -16) | ((me - 1) & 15)
    east = (me & -16) | ((me + 1) & 15)
    one_hot = [(tiles == t).astype(F32).astype(BF16) for t in (me, west, east)]

    def pick(which, lo, hi):
        a, b, c = three_parts(xs_ref[:, lo:hi])
        m = one_hot[which]
        return (dot(m, c) + dot(m, b)) + dot(m, a)

    base = LINES * 128
    halo = pick(1, base, base + 128) + pick(2, base + 128, base + 256)
    odd = lax.rem(reader, 2) == 1
    for block in range(LINES // 2):
        t = pick(0, block * 256, block * 256 + 256)
        for k in range(2):
            line = 2 * block + k
            part = t[:, k * 128 : k * 128 + 128]
            if line == 0:
                part = part + jnp.where(odd, halo, 0.0)
            if line == LINES - 1:
                part = part + jnp.where(odd, 0.0, halo)
            for g in range(16):
                out_ref[pl.ds(8 * LINES * g + line, 8, stride=LINES), :] = part[8 * g : 8 * g + 8]


def north_rows():
    for s in range(2 + 1):
        for f in range(3):
            n = (2, 3, 2)[f] - s
            for l in range(LEV - (f == 2)):
                if n > 0:
                    yield s, f, l, n


def south_rows():
    for s in range(2):
        for f in range(3):
            for l in range(LEV - (f == 2)):
                yield s, f, l, 2 - s


NORTH = 3 * sum(r[3] for r in north_rows())
SOUTH = 3 * sum(r[3] for r in south_rows())


def unpack(lines_ref, flat_ref, edge_ref):
    lane = lane_iota()
    for p in range(64):
        a, b = 27 * p, 28 * p
        for to, frm in ((0, 0), (5, 5), (14, 15), (19, 20)):
            flat_ref[a + to : a + to + 8, :] = lines_ref[b + frm : b + frm + 8, :]
        flat_ref[a + 13 : a + 14, :] = jnp.where(
            lane[:1] < 64, lines_ref[b + 13 : b + 14, :], lines_ref[b + 14 : b + 15, :]
        )
    for gg in range(4):
        spare = [
            lines_ref[pl.ds(448 * gg + off, 8, stride=56), :] for off in (13, 14, 41, 42)
        ]
        for n in range(27):
            i, j = divmod(n, 7)
            right = pltpu.roll(spare[i], (128 - ((64, 0)[i % 2] + 8 * j)) % 128, 1)
            i, j = divmod(n + 1, 7)
            left = pltpu.roll(spare[i], (128 - ((64, 0)[i % 2] + 8 * j + 8)) % 128, 1)
            edge_ref[pl.ds(216 * gg + n, 8, stride=27), :] = jnp.where(lane < 64, right, left)


def edge_rows_kernel(lines_ref, west_ref, east_ref, north_ref, south_ref, flat_ref, edge_ref):
    unpack(lines_ref, flat_ref, edge_ref)
    at = 0
    for s, f, l, n in north_rows():
        q = (s * 3 + f) * LEV + l
        for h in range(2):
            north_ref[at : at + n, :] = flat_ref[pl.ds(32 * q + 2 * (CY - n) + h, n, stride=2), :]
            at += n
        north_ref[at : at + n, :] = edge_ref[16 * q + CY - n : 16 * q + CY, :]
        at += n
    at = 0
    for s, f, l, n in south_rows():
        q = (s * 3 + f) * LEV + l
        for h in range(2):
            south_ref[at : at + n, :] = flat_ref[pl.ds(32 * q + h, n, stride=2), :]
            at += n
        south_ref[at : at + n, :] = edge_ref[16 * q : 16 * q + n, :]
        at += n
    k = 0
    for ref in (west_ref, east_ref):
        for half in range(2):
            north_ref[NORTH + k : NORTH + k + 3, :] = ref[16 * half + 13 : 16 * half + 16, :]
            south_ref[SOUTH + k : SOUTH + k + 3, :] = ref[16 * half : 16 * half + 3, :]
            k += 3


def field(tracers_ref, ocean_ref, f, rows, cols):
    if f < NTR * LEV:
        l, c = divmod(f, NTR)
        return tracers_ref[c, l, rows, cols]
    return ocean_ref[rows, cols].astype(F32)


def ends_kernel(tracers_ref, ocean_ref, north_ref, south_ref, east_ref, west_ref):
    lane = lane_iota()
    for f in range(NF):
        for h in range(2):
            cols = slice(128 * h, 128 * h + 128)
            at = (f * 2 + h) * 3
            north_ref[at : at + 3, :] = field(tracers_ref, ocean_ref, f, slice(CY - 3, CY), cols)
            south_ref[at : at + 3, :] = field(tracers_ref, ocean_ref, f, slice(0, 3), cols)
    for half in range(2):
        for g in range(2):
            rows = slice(8 * g, 8 * g + 8)
            east = jnp.zeros((8, 128), F32)
            west = jnp.zeros((8, 128), F32)
            for f in range(32 * half, min(32 * half + 32, NF)):
                m = 4 * (f % 32)
                use = (lane >= m) & (lane < m + 3)
                last = field(tracers_ref, ocean_ref, f, rows, slice(128, 256))
                first = field(tracers_ref, ocean_ref, f, rows, slice(0, 128))
                east = jnp.where(use, pltpu.roll(last, (m + 3) % 128, 1), east)
                west = jnp.where(use, pltpu.roll(first, m, 1) if m else first, west)
            to = 16 * half + 8 * g
            east_ref[to : to + 8, :] = east
            west_ref[to : to + 8, :] = west


def fill_frames(
    tracers_ref, ocean_ref, below_ref, above_ref, west_ref, east_ref, f_below_ref, f_above_ref,
    main_ref, side_ref, ends_ref,
):
    zero = jnp.zeros((4, 128), F32)
    for f in range(NF):
        for h in range(2):
            cols = slice(128 * h, 128 * h + 128)
            at, frm = (f * 2 + h) * FR, (f * 2 + h) * 3
            main_ref[at : at + 3, :] = below_ref[frm : frm + 3, :]
            for g in range(2):
                main_ref[at + 3 + 8 * g : at + 11 + 8 * g, :] = field(
                    tracers_ref, ocean_ref, f, slice(8 * g, 8 * g + 8), cols
                )
            main_ref[at + 19 : at + 22, :] = above_ref[frm : frm + 3, :]
            main_ref[at + 22 : at + 26, :] = zero
    for k in range(4):
        ref, half, to = (west_ref, east_ref)[k // 2], k % 2, 24 * k
        ends_ref[to : to + 3, :] = f_below_ref[NORTH + 3 * k : NORTH + 3 * k + 3, :]
        ends_ref[to + 3 : to + 11, :] = ref[16 * half : 16 * half + 8, :]
        ends_ref[to + 11 : to + 19, :] = ref[16 * half + 8 : 16 * half + 16, :]
        ends_ref[to + 19 : to + 22, :] = f_above_ref[SOUTH + 3 * k : SOUTH + 3 * k + 3, :]
        ends_ref[to + 22 : to + 24, :] = zero[:2]
    lane = lane_iota()
    for f in range(NF):
        m = 4 * (f % 32)
        frm = 24 * (f // 32)
        for g in range(3):
            right = ends_ref[48 + frm + 8 * g : 56 + frm + 8 * g, :]
            if m:
                right = pltpu.roll(right, 128 - m, 1)
            left = pltpu.roll(ends_ref[frm + 8 * g : frm + 8 * g + 8, :], 125 - m, 1)
            side_ref[f * FR + 8 * g : f * FR + 8 * g + 8, :] = jnp.where(lane < 64, right, left)
        side_ref[f * FR + 24 : f * FR + 26, :] = zero[:2]


def shift_east(tiles, lane):
    moved = [pltpu.roll(t, 127, 1) for t in tiles]
    n = len(tiles)
    return [jnp.where(lane == 127, moved[(h + 1) % n], moved[h]) for h in range(n)]


def shift_west(tiles, lane):
    moved = [pltpu.roll(t, 1, 1) for t in tiles]
    n = len(tiles)
    return [jnp.where(lane == 0, moved[(h - 1) % n], moved[h]) for h in range(n)]


def transport_kernel(
    tracers_ref,
    ocean_ref,
    t_below_ref,
    t_above_ref,
    west_ref,
    east_ref,
    rates_ref,
    lines_ref,
    below_ref,
    above_ref,
    hot_hbm_ref,
    yrow_ref,
    out_ref,
    picked_ref,
    flat_ref,
    edge_ref,
    u_ref,
    v_ref,
    k_ref,
    main_ref,
    side_ref,
    ends_ref,
    main1_ref,
    side1_ref,
    main2_ref,
    side2_ref,
    coef_ref,
    env_ref,
    lhs_ref,
    hot_ref,
    hot_sem,
):
    hot_copy = pltpu.make_async_copy(hot_hbm_ref, hot_ref, hot_sem)
    hot_copy.start()
    fill_frames(
        tracers_ref, ocean_ref, t_below_ref, t_above_ref, west_ref, east_ref, below_ref, above_ref,
        main_ref, side_ref, ends_ref,
    )
    lane = lane_iota()
    unpack(lines_ref, flat_ref, edge_ref)

    below, above = {}, {}
    at = 0
    for s, f, l, n in north_rows():
        below[s, f, l] = (at, n)
        at += 3 * n
    at = 0
    for s, f, l, n in south_rows():
        above[s, f, l] = (at, n)
        at += 3 * n
    for s in range(SUBS):
        for f in range(3):
            ref = (u_ref, v_ref, k_ref)[f]
            for l in range(LEV - (f == 2)):
                q = (s * 3 + f) * LEV + l
                k = s * LEV + l if f < 2 else s * (LEV + 1) + l + 1
                for h in range(3):
                    to = (k * 3 + h) * FR
                    for g in range(2):
                        if h < 2:
                            part = flat_ref[pl.ds(32 * q + 16 * g + h, 8, stride=2), :]
                        else:
                            part = edge_ref[16 * q + 8 * g : 16 * q + 8 * g + 8, :]
                        ref[to + 3 + 8 * g : to + 11 + 8 * g, :] = part
                    if (s, f, l) in below:
                        frm, n = below[s, f, l]
                        ref[to + 3 - n : to + 3, :] = below_ref[frm + h * n : frm + h * n + n, :]
                    if (s, f, l) in above:
                        frm, n = above[s, f, l]
                        ref[to + 19 : to + 19 + n, :] = above_ref[frm + h * n : frm + h * n + n, :]
        for k in (s * (LEV + 1), s * (LEV + 1) + LEV):
            for r in range(0, 3 * FR, 6):
                k_ref[k * 3 * FR + r : k * 3 * FR + r + 6, :] = jnp.zeros((6, 128), F32)

    def substep(s, src, dst):
        start = 1 if s < 2 else 3
        groups = 3 if s < 2 else 2
        width = 3 if s < 2 else 2
        smain, sside = src

        def body(t, _):
            l = lax.div(t, groups)
            g = lax.rem(t, groups)
            row = start + 8 * g

            def frame(f, h, off=0):
                if h < 2:
                    return smain[pl.ds((f * 2 + h) * FR + row + off, 8), :]
                return sside[pl.ds(f * FR + row + off, 8), :]

            def forcing(ref, k, h, off=0):
                return ref[pl.ds((k * 3 + h) * FR + row + off, 8), :]

            def ocean(h, off=0):
                f = NTR * LEV
                if h < 2:
                    return main_ref[pl.ds((f * 2 + h) * FR + row + off, 8), :]
                return side_ref[pl.ds(f * FR + row + off, 8), :]

            o = [ocean(h) for h in range(3)]
            u = [forcing(u_ref, s * LEV + l, h) for h in range(3)]
            open_east = [a * b for a, b in zip(o, shift_east(o, lane))]
            up = [w * jnp.maximum(x, 0.0) for w, x in zip(open_east, u)]
            um = [w * jnp.minimum(x, 0.0) for w, x in zip(open_east, u)]
            up_w, um_w = shift_west(up, lane), shift_west(um, lane)
            for h in range(width):
                v = forcing(v_ref, s * LEV + l, h)
                v_s = forcing(v_ref, s * LEV + l, h, -1)
                open_n, open_s = o[h] * ocean(h, 1), o[h] * ocean(h, -1)
                vp, vm = open_n * jnp.maximum(v, 0.0), open_n * jnp.minimum(v, 0.0)
                vp_s, vm_s = open_s * jnp.maximum(v_s, 0.0), open_s * jnp.minimum(v_s, 0.0)
                k_up = o[h] * forcing(k_ref, s * (LEV + 1) + l + 1, h)
                k_dn = o[h] * forcing(k_ref, s * (LEV + 1) + l, h)
                own = (um_w[h] - up[h]) + (vm_s - vp) - (k_up + k_dn)
                own = own + 1.0
                values = (own, -um[h], up_w[h], -vm, vp_s, k_up, k_dn, o[h])
                for i, value in enumerate(values):
                    coef_ref[(h * 8 + i) * 8 : (h * 8 + i) * 8 + 8, :] = value

            def coef(h, i):
                return coef_ref[(h * 8 + i) * 8 : (h * 8 + i) * 8 + 8, :]

            l_up, l_dn = jnp.minimum(l + 1, LEV - 1), jnp.maximum(l - 1, 0)
            cells = [[frame(l * NTR + c, h) for h in range(3)] for c in range(NTR)]
            for a in range(NTR):
                f = l * NTR + a
                rate = rates_ref[a * NTR]
                grown = [rate * cells[0][h] for h in range(width)]
                for b in range(1, NTR):
                    rate = rates_ref[a * NTR + b]
                    grown = [grown[h] + rate * cells[b][h] for h in range(width)]
                east, west = shift_east(cells[a], lane), shift_west(cells[a], lane)
                for h in range(width):
                    value = coef(h, 0) * cells[a][h] + coef(h, 7) * grown[h]
                    value = value + coef(h, 1) * east[h] + coef(h, 2) * west[h]
                    value = value + coef(h, 3) * frame(f, h, 1) + coef(h, 4) * frame(f, h, -1)
                    value = value + coef(h, 5) * frame(l_up * NTR + a, h)
                    value = value + coef(h, 6) * frame(l_dn * NTR + a, h)
                    if s == 2:
                        rows = pl.ds(pl.multiple_of(8 * g, 8), 8)
                        out_ref[a, l, rows, 128 * h : 128 * h + 128] = value
                        env_ref[h, pl.ds((a * LEV + l) * CY + 8 * g, 8), :] = value
                    elif h < 2:
                        dst[0][pl.ds((f * 2 + h) * FR + row, 8), :] = value
                    else:
                        dst[1][pl.ds(f * FR + row, 8), :] = value
            return 0

        lax.fori_loop(0, groups * LEV, body, 0)

    substep(0, (main_ref, side_ref), (main1_ref, side1_ref))
    substep(1, (main1_ref, side1_ref), (main2_ref, side2_ref))
    substep(2, (main2_ref, side2_ref), None)

    env_ref[:, NTR * LEV * CY :, :] = jnp.zeros((2, 4 * CY, 128), F32)
    for y in range(CY):
        for h in range(2):
            part = [env_ref[h, pl.ds(128 * k + y, 8, stride=CY), :] for k in range(8)]
            x = jnp.concatenate(part, axis=0)
            hi = x.astype(BF16)
            lo = (x - hi.astype(F32)).astype(BF16)
            lhs_ref[128 * y : 128 * y + 64, 128 * h : 128 * h + 128] = hi
            lhs_ref[128 * y + 64 : 128 * y + 128, 128 * h : 128 * h + 128] = lo

    hot_copy.wait()

    def slots(n, _):
        cols = pl.ds(pl.multiple_of(256 * n, 256), 256)
        found = dot(lhs_ref[...], hot_ref[:, cols])
        row = yrow_ref[0:1, cols]
        total = jnp.where(row == 0, found[:128], 0.0)
        for y in range(1, CY):
            total = total + jnp.where(row == y, found[128 * y : 128 * y + 128], 0.0)
        picked_ref[:, cols] = total.astype(BF16)
        return 0

    lax.fori_loop(0, 8, slots, 0)


def slots_kernel(cells_ref, hot_ref, yrow_ref):
    own = lax.axis_index("lon")
    column = lax.broadcasted_iota(jnp.int32, (256, 128), 0)
    for n in range(16):
        cell = cells_ref[0, n, pl.ds(own, 1), :]
        hot_ref[:, 128 * n : 128 * n + 128] = ((cell & 255) == column).astype(F32).astype(BF16)
        yrow_ref[:, 128 * n : 128 * n + 128] = lax.shift_right_logical(cell, 8)


def agents_kernel(traits_ref, picked_ref, tw_ref, ew_ref, counts_ref, out_ref, weights_ref):
    own = lax.axis_index("lon")
    ew = jnp.concatenate([ew_ref[...], jnp.zeros((4, 64), F32)], axis=0)
    for k, w in enumerate((tw_ref[...], ew)):
        w = w.T
        hi = w.astype(BF16)
        lo = (w - hi.astype(F32)).astype(BF16)
        for i, part in enumerate((hi, hi, lo)):
            weights_ref[:, (3 * k + i) * 64 : (3 * k + i) * 64 + 64] = part
    slot = lax.broadcasted_iota(jnp.int32, (64, 128), 1)
    for n in range(0, 16, 2):
        x = jnp.concatenate([traits_ref[n], traits_ref[n + 1]], axis=1)
        hi = x.astype(BF16)
        lo = (x - hi.astype(F32)).astype(BF16)
        picked = picked_ref[:, 128 * n : 128 * n + 256]
        rhs = jnp.concatenate([hi, lo, hi, picked, picked[:64]], axis=0)
        new = x + jnp.tanh(dot(weights_ref[...], rhs))
        for k in range(2):
            live = slot < counts_ref[0, n + k, own]
            out_ref[n + k] = jnp.where(live, new[:, 128 * k : 128 * k + 128], 0.0)


def shards(
    tracers,
    forcing_groups,
    group_tiles,
    ocean_mask,
    bio_rates,
    agent_traits,
    agent_cells,
    agent_counts,
    trait_weights,
    env_weights,
):
    north = [(i, i + 1) for i in range(7)]
    south = [(i + 1, i) for i in range(7)]
    east = [(i, (i + 1) % 16) for i in range(16)]
    west = [((i + 1) % 16, i) for i in range(16)]

    vmem = pl.BlockSpec(memory_space=pltpu.VMEM)
    hbm = pl.BlockSpec(memory_space=pltpu.HBM)

    lines = call(
        sort_bands_kernel,
        full(128 * LINES, 128),
        [pltpu.VMEM((128, LINES * 128 + 256), F32)],
    )(forcing_groups, group_tiles)
    lines = lines.reshape(128, 1, LINES * 128)
    lines = lax.all_to_all(lines, ("lat", "lon"), split_axis=0, concat_axis=0, tiled=True)
    lines = lines.reshape(128 * LINES, 128)

    n_rows, n_cols = full(NF * 6, 128), full(32, 128)
    to_north, to_south, to_east, to_west = call(ends_kernel, (n_rows, n_rows, n_cols, n_cols))(
        tracers, ocean_mask
    )
    below = lax.ppermute(to_north, "lat", north)
    above = lax.ppermute(to_south, "lat", south)
    from_west = lax.ppermute(to_east, "lon", east)
    from_east = lax.ppermute(to_west, "lon", west)
    rates = jnp.broadcast_to((BIO_STEP * bio_rates).reshape(NTR * NTR, 1, 1), (NTR * NTR, 8, 128))
    hot, yrow = call(
        slots_kernel, (full(256, 2048, dtype=BF16), full(1, 2048, dtype=jnp.int32))
    )(agent_cells)
    lines, below, above, from_west, from_east, hot, yrow, rates = lax.optimization_barrier(
        (lines, below, above, from_west, from_east, hot, yrow, rates)
    )
    f_north, f_south = call(
        edge_rows_kernel,
        (full(NORTH + 12, 128), full(SOUTH + 12, 128)),
        [pltpu.VMEM((1728, 128), F32), pltpu.VMEM((864, 128), F32)],
    )(lines, from_west, from_east)
    f_below = lax.ppermute(f_north, "lat", north)
    f_above = lax.ppermute(f_south, "lat", south)
    traits, _ = lax.optimization_barrier((agent_traits[0, 0], f_north))
    received = lax.all_to_all(traits, "lon", split_axis=0, concat_axis=0, tiled=True)

    n_main, n_side = NTR * LEV * 2 * FR, NTR * LEV * FR
    tracers_out, picked = call(
        transport_kernel,
        (full(NTR, LEV, CY, CX), full(128, 2048, dtype=BF16)),
        [
            pltpu.VMEM((1728, 128), F32),
            pltpu.VMEM((864, 128), F32),
            pltpu.VMEM((SUBS * LEV * 3 * FR, 128), F32),
            pltpu.VMEM((SUBS * LEV * 3 * FR, 128), F32),
            pltpu.VMEM((SUBS * (LEV + 1) * 3 * FR, 128), F32),
            pltpu.VMEM((NF * 2 * FR, 128), F32),
            pltpu.VMEM((NF * FR, 128), F32),
            pltpu.VMEM((96, 128), F32),
            pltpu.VMEM((n_main, 128), F32),
            pltpu.VMEM((n_side, 128), F32),
            pltpu.VMEM((n_main, 128), F32),
            pltpu.VMEM((n_side, 128), F32),
            pltpu.VMEM((3 * 8 * 8, 128), F32),
            pltpu.VMEM((2, 64 * CY, 128), F32),
            pltpu.VMEM((128 * CY, 256), BF16),
            pltpu.VMEM((256, 2048), BF16),
            pltpu.SemaphoreType.DMA,
        ],
        limit=20,
        in_specs=[vmem] * 10 + [hbm, vmem],
        flops=BUSY,
    )(tracers, ocean_mask, below, above, from_west, from_east, rates, lines, f_below, f_above, pltpu.with_memory_space_constraint(hot, pltpu.HBM), yrow)

    agent_state = call(
        agents_kernel,
        full(16, 64, 128),
        [pltpu.VMEM((64, 384), BF16)],
        in_specs=[vmem] * 4 + [pl.BlockSpec(memory_space=pltpu.SMEM)],
    )(received, picked, trait_weights, env_weights, agent_counts)
    return (tracers_out, agent_state[None, None])


def solution(mesh):
    placed = (
        P(None, None, "lat", "lon"),
        P(("lat", "lon"), None, None),
        P(("lat", "lon"), None),
        P("lat", "lon"),
        P(),
        P("lat", "lon", None, None, None),
        P("lat", None, None, None),
        P("lat", None, None),
        P(),
        P(),
    )
    return jax.shard_map(
        shards,
        mesh=mesh,
        in_specs=placed,
        out_specs=(P(None, None, "lat", "lon"), P("lat", "lon", None, None, None)),
        check_vma=False,
    )
```

profile of v0, /device:TPU:1, one launch (start us, length us, event | category | flops | bytes accessed | tf_op | source)
XLA Modules:
  0.0 63.9 jit_solution(3826442417770991232)
XLA Ops:
  0.6 1.5 %copy.13.bands_ref = f32[1,128,1728]{2,1,0:T(8,128)S(1)} copy(f32[1,128,1728]{1,2,0:T(8,128)} %param.11) | data formatting | bytes 1769472 | tf_op args[1]
  2.1 1.8 %shard_map.113 = f32[1792,128]{1,0:T(8,128)} custom-call(f32[1,128,1728]{2,1,0:T(8,128)S(1)} %copy.13.bands_ref, s32[1,128]{1,0:T(1,128)S(1)} %copy-done.6), custom_call_target="tpu_custom_call" | custom-call | tf_op jit(solution)/shard_map/pallas_call | solution.py:496
  3.9 12.1 %all-to-all-start = ((f32[128,1,1792]{2,1,0:T(1,128)}), f32[128,1,1792]{2,1,0:T(1,128)S(1)}, u32[]{:S(2)}, u32[]{:S(2)}) async-start(f32[128,1,1792]{2,1,0:T(1,128)} %bitcast), calls=%async_computation | async-start | bytes 1835008 | tf_op jit(solution)/shard_map/all_to_all | solution.py:502
  16.1 0.0 copy-start.8
  16.1 0.4 shard_map.114
  16.5 3.5 %collective-permute-start = (f32[366,128]{1,0:T(8,128)S(1)}, f32[366,128]{1,0:T(8,128)S(1)}, u32[]{:S(2)}, u32[]{:S(2)}) collective-permute-start(f32[366,128]{1,0:T(8,128)S(1)} %get-tuple-element.21), channel_id=1, source_target_pairs={{0,16},{16,32},{32,48},{48,64},{64,80},{80,96},{96,112},{1,17},{17... | collective-permute-start | bytes 562184 | tf_op jit(solution)/shard_map/ppermute | solution.py:509
  20.0 1.9 %collective-permute-start.1 = (f32[366,128]{1,0:T(8,128)S(1)}, f32[366,128]{1,0:T(8,128)S(1)}, u32[]{:S(2)}, u32[]{:S(2)}) collective-permute-start(f32[366,128]{1,0:T(8,128)S(1)} %get-tuple-element.22), channel_id=1, source_target_pairs={{16,0},{32,16},{48,32},{64,48},{80,64},{96,80},{112,96},{17,1},{33... | collective-permute-start | bytes 562184 | tf_op jit(solution)/shard_map/ppermute | solution.py:510
  22.0 1.4 %collective-permute-start.2 = (f32[32,128]{1,0:T(8,128)S(1)}, f32[32,128]{1,0:T(8,128)S(1)}, u32[]{:S(2)}, u32[]{:S(2)}) collective-permute-start(f32[32,128]{1,0:T(8,128)S(1)} %get-tuple-element.23), channel_id=1, source_target_pairs={{0,1},{1,2},{2,3},{3,4},{4,5},{5,6},{6,7},{7,8},{8,9},{9,10},{10,1... | collective-permute-start | bytes 49160 | tf_op jit(solution)/shard_map/ppermute | solution.py:511
  23.4 4.1 %collective-permute-start.3 = (f32[32,128]{1,0:T(8,128)S(1)}, f32[32,128]{1,0:T(8,128)S(1)}, u32[]{:S(2)}, u32[]{:S(2)}) collective-permute-start(f32[32,128]{1,0:T(8,128)S(1)} %get-tuple-element.24), channel_id=1, source_target_pairs={{1,0},{2,1},{3,2},{4,3},{5,4},{6,5},{7,6},{8,7},{9,8},{10,9},{11,1... | collective-permute-start | bytes 49160 | tf_op jit(solution)/shard_map/ppermute | solution.py:512
  27.5 0.3 shard_map.115
  27.8 1.0 %copy-done.7 = bf16[256,2048]{1,0:T(8,128)(2,1)} copy-done((bf16[256,2048]{1,0:T(8,128)(2,1)}, bf16[256,2048]{1,0:T(8,128)(2,1)S(1)}, u32[]{:S(2)}) %copy-start.7) | copy-done | bytes 1048600
  28.8 0.1 broadcast_in_dim.10
  28.9 0.8 %collective-permute-done.2.west_ref = f32[32,128]{1,0:T(8,128)S(1)} collective-permute-done((f32[32,128]{1,0:T(8,128)S(1)}, f32[32,128]{1,0:T(8,128)S(1)}, u32[]{:S(2)}, u32[]{:S(2)}) %collective-permute-start.2) | collective-permute-done | bytes 16416 | tf_op jit(solution)/shard_map/ppermute | solution.py:511
  29.7 0.2 collective-permute-done.1.t_above_ref
  29.9 3.9 %all-to-all-done = f32[128,1,1792]{2,1,0:T(1,128)S(1)} async-done(((f32[128,1,1792]{2,1,0:T(1,128)}), f32[128,1,1792]{2,1,0:T(1,128)S(1)}, u32[]{:S(2)}, u32[]{:S(2)}) %all-to-all-start) | async-done | bytes 917536 | tf_op jit(solution)/shard_map/all_to_all | solution.py:502
  33.8 0.2 broadcast_in_dim.11.rates_ref
  33.9 0.3 shard_map.116
  34.2 3.3 %collective-permute-start.4 = (f32[219,128]{1,0:T(8,128)S(1)}, f32[219,128]{1,0:T(8,128)S(1)}, u32[]{:S(2)}, u32[]{:S(2)}) collective-permute-start(f32[219,128]{1,0:T(8,128)S(1)} %get-tuple-element.33), channel_id=1, source_target_pairs={{0,16},{16,32},{32,48},{48,64},{64,80},{80,96},{96,112},{1,17},{17... | collective-permute-start | bytes 336392 | tf_op jit(solution)/shard_map/ppermute | solution.py:525
  37.5 1.9 %collective-permute-start.5 = (f32[165,128]{1,0:T(8,128)S(1)}, f32[165,128]{1,0:T(8,128)S(1)}, u32[]{:S(2)}, u32[]{:S(2)}) collective-permute-start(f32[165,128]{1,0:T(8,128)S(1)} %get-tuple-element.34), channel_id=1, source_target_pairs={{16,0},{32,16},{48,32},{64,48},{80,64},{96,80},{112,96},{17,1},{33... | collective-permute-start | bytes 253448 | tf_op jit(solution)/shard_map/ppermute | solution.py:526
  39.4 4.3 %all-to-all-start.1 = ((f32[16,64,128]{2,1,0:T(8,128)}), f32[16,64,128]{2,1,0:T(8,128)}, u32[]{:S(2)}, u32[]{:S(2)}) async-start(f32[16,64,128]{2,1,0:T(8,128)} %bitcast.7), calls=%async_computation.1 | async-start | bytes 1048576 | tf_op jit(solution)/shard_map/all_to_all | solution.py:528
  43.7 0.0 copy-start.3
  43.7 0.0 copy-start.5
  43.7 17.8 %shard_map.117 = (f32[10,6,16,256]{3,2,1,0:T(8,128)}, bf16[128,2048]{1,0:T(8,128)(2,1)S(1)}) custom-call(f32[10,6,16,256]{3,2,1,0:T(8,128)S(1)} %copy-done, s32[16,256]{1,0:T(8,128)S(1)} %copy-done.4, f32[366,128]{1,0:T(8,128)S(1)} %collective-permute-done.t_below_ref, f32[366,128]{1,0:T(8,128)S(1)} %collective-permute-done.1.t_above_ref, ...), custom_call_target="tpu_custom_call" | custom-call | flops 999999995904 | tf_op jit(solution)/shard_map/pallas_call | solution.py:531
  61.5 2.4 %shard_map.118 = f32[16,64,128]{2,1,0:T(8,128)} custom-call(f32[16,64,128]{2,1,0:T(8,128)} %all-to-all-done.1.traits_ref, bf16[128,2048]{1,0:T(8,128)(2,1)S(1)} %get-tuple-element.39.picked_ref, f32[64,64]{1,0:T(8,128)S(1)} %copy-done.2, f32[60,64]{1,0:T(8,128)S(1)} %copy-done.3, s32[1,16,16]{2,1,0:T(8,128)S(1)} %copy-done.5), custom_call_target="tpu_custom_call" | custom-call | tf_op jit(solution)/shard_map/pallas_call | solution.py:558
  (20 shorter events, 0.0 us)
Async XLA Ops:
  0.6 1.5 %copy-start.6 = (s32[1,128]{1,0:T(1,128)S(1)}, s32[1,128]{1,0:T(1,128)}, u32[]{:S(2)}) copy-start(s32[1,128]{1,0:T(1,128)} %tiles_ref.1) | copy-start | bytes 1540
  3.9 12.1 %copy-start = (f32[10,6,16,256]{3,2,1,0:T(8,128)S(1)}, f32[10,6,16,256]{3,2,1,0:T(8,128)}, u32[]{:S(2)}) copy-start(f32[10,6,16,256]{3,2,1,0:T(8,128)} %tracers_ref.3) | copy-start | bytes 2949124
  3.9 12.1 %copy-start.4 = (s32[16,256]{1,0:T(8,128)S(1)}, s32[16,256]{1,0:T(8,128)}, u32[]{:S(2)}) copy-start(s32[16,256]{1,0:T(8,128)} %ocean_ref.3) | copy-start | bytes 49156
  3.9 29.8 %all-to-all-start = ((f32[128,1,1792]{2,1,0:T(1,128)}), f32[128,1,1792]{2,1,0:T(1,128)S(1)}, u32[]{:S(2)}, u32[]{:S(2)}) async-start(f32[128,1,1792]{2,1,0:T(1,128)} %bitcast), calls=%async_computation | async-start | bytes 1835008 | tf_op jit(solution)/shard_map/all_to_all | solution.py:502
  16.1 11.4 %copy-start.8 = (f32[10,10]{1,0:T(8,128)S(1)}, f32[10,10]{1,0:T(8,128)}, u32[]{:S(2)}) copy-start(f32[10,10]{1,0:T(8,128)} %param.14) | copy-start | bytes 1204
  16.1 11.4 %copy-start.1 = (s32[1,16,16,128]{3,2,1,0:T(8,128)S(1)}, s32[1,16,16,128]{3,2,1,0:T(8,128)}, u32[]{:S(2)}) copy-start(s32[1,16,16,128]{3,2,1,0:T(8,128)} %cells_ref.1) | copy-start | bytes 393220
  16.5 13.2 %collective-permute-start = (f32[366,128]{1,0:T(8,128)S(1)}, f32[366,128]{1,0:T(8,128)S(1)}, u32[]{:S(2)}, u32[]{:S(2)}) collective-permute-start(f32[366,128]{1,0:T(8,128)S(1)} %get-tuple-element.21), channel_id=1, source_target_pairs={{0,16},{16,32},{32,48},{48,64},{64,80},{80,96},{96,112},{1,17},{17... | collective-permute-start | bytes 562184 | tf_op jit(solution)/shard_map/ppermute | solution.py:509
  20.0 9.9 %collective-permute-start.1 = (f32[366,128]{1,0:T(8,128)S(1)}, f32[366,128]{1,0:T(8,128)S(1)}, u32[]{:S(2)}, u32[]{:S(2)}) collective-permute-start(f32[366,128]{1,0:T(8,128)S(1)} %get-tuple-element.22), channel_id=1, source_target_pairs={{16,0},{32,16},{48,32},{64,48},{80,64},{96,80},{112,96},{17,1},{33... | collective-permute-start | bytes 562184 | tf_op jit(solution)/shard_map/ppermute | solution.py:510
  22.0 7.7 %collective-permute-start.2 = (f32[32,128]{1,0:T(8,128)S(1)}, f32[32,128]{1,0:T(8,128)S(1)}, u32[]{:S(2)}, u32[]{:S(2)}) collective-permute-start(f32[32,128]{1,0:T(8,128)S(1)} %get-tuple-element.23), channel_id=1, source_target_pairs={{0,1},{1,2},{2,3},{3,4},{4,5},{5,6},{6,7},{7,8},{8,9},{9,10},{10,1... | collective-permute-start | bytes 49160 | tf_op jit(solution)/shard_map/ppermute | solution.py:511
  23.4 6.3 %collective-permute-start.3 = (f32[32,128]{1,0:T(8,128)S(1)}, f32[32,128]{1,0:T(8,128)S(1)}, u32[]{:S(2)}, u32[]{:S(2)}) collective-permute-start(f32[32,128]{1,0:T(8,128)S(1)} %get-tuple-element.24), channel_id=1, source_target_pairs={{1,0},{2,1},{3,2},{4,3},{5,4},{6,5},{7,6},{8,7},{9,8},{10,9},{11,1... | collective-permute-start | bytes 49160 | tf_op jit(solution)/shard_map/ppermute | solution.py:512
  27.8 1.0 %copy-start.7 = (bf16[256,2048]{1,0:T(8,128)(2,1)}, bf16[256,2048]{1,0:T(8,128)(2,1)S(1)}, u32[]{:S(2)}) copy-start(bf16[256,2048]{1,0:T(8,128)(2,1)S(1)} %get-tuple-element.35.hot_hbm_ref) | copy-start | bytes 3145732
  34.2 9.5 %collective-permute-start.4 = (f32[219,128]{1,0:T(8,128)S(1)}, f32[219,128]{1,0:T(8,128)S(1)}, u32[]{:S(2)}, u32[]{:S(2)}) collective-permute-start(f32[219,128]{1,0:T(8,128)S(1)} %get-tuple-element.33), channel_id=1, source_target_pairs={{0,16},{16,32},{32,48},{48,64},{64,80},{80,96},{96,112},{1,17},{17... | collective-permute-start | bytes 336392 | tf_op jit(solution)/shard_map/ppermute | solution.py:525
  37.5 6.2 %collective-permute-start.5 = (f32[165,128]{1,0:T(8,128)S(1)}, f32[165,128]{1,0:T(8,128)S(1)}, u32[]{:S(2)}, u32[]{:S(2)}) collective-permute-start(f32[165,128]{1,0:T(8,128)S(1)} %get-tuple-element.34), channel_id=1, source_target_pairs={{16,0},{32,16},{48,32},{64,48},{80,64},{96,80},{112,96},{17,1},{33... | collective-permute-start | bytes 253448 | tf_op jit(solution)/shard_map/ppermute | solution.py:526
  39.4 22.1 %all-to-all-start.1 = ((f32[16,64,128]{2,1,0:T(8,128)}), f32[16,64,128]{2,1,0:T(8,128)}, u32[]{:S(2)}, u32[]{:S(2)}) async-start(f32[16,64,128]{2,1,0:T(8,128)} %bitcast.7), calls=%async_computation.1 | async-start | bytes 1048576 | tf_op jit(solution)/shard_map/all_to_all | solution.py:528
  43.7 17.8 %copy-start.2 = (f32[64,64]{1,0:T(8,128)S(1)}, f32[64,64]{1,0:T(8,128)}, u32[]{:S(2)}) copy-start(f32[64,64]{1,0:T(8,128)} %tw_ref.1) | copy-start | bytes 49156
  43.7 17.8 %copy-start.3 = (f32[60,64]{1,0:T(8,128)S(1)}, f32[60,64]{1,0:T(8,128)}, u32[]{:S(2)}) copy-start(f32[60,64]{1,0:T(8,128)} %ew_ref.1) | copy-start | bytes 46084
  43.7 17.8 %copy-start.5 = (s32[1,16,16]{2,1,0:T(8,128)S(1)}, s32[1,16,16]{2,1,0:T(8,128)}, u32[]{:S(2)}) copy-start(s32[1,16,16]{2,1,0:T(8,128)} %counts_ref.1) | copy-start | bytes 3076
where the time goes:
time: 64.3 us; the launch traced here: 63.9 us
  starting transfers between devices  32.5 us (51%)
  Pallas kernels  22.9 us (36%)
  waiting for transfers between devices  4.9 us (8%)
  local copies, waits for them, and re-layouts  2.74 us (4%)
  between operations  0.86 us (1%)
    pallas_call x1, Pallas kernels, shards(): call(transport_kernel, (full(NTR, LEV, CY, CX), full(128, 2048, dtype=BF1...  17.8 us
    all_to_all x1, starting transfers between devices, shards(): lax.all_to_all(lines, ('lat', 'lon'), split_axis=0, concat_axis=0, tiled=...  12.1 us
    all_to_all x1, starting transfers between devices, shards(): lax.all_to_all(traits, 'lon', split_axis=0, concat_axis=0, tiled=True)  4.26 us
    ppermute x1, starting transfers between devices, shards(): from_east = lax.ppermute(to_west, 'lon', west)  4.14 us
    all_to_all x1, waiting for transfers between devices, shards(): lax.all_to_all(lines, ('lat', 'lon'), split_axis=0, concat_axis=0, tiled=...  3.87 us
    ppermute x1, starting transfers between devices, shards(): below = lax.ppermute(to_north, 'lat', north)  3.54 us
    ppermute x1, starting transfers between devices, shards(): f_below = lax.ppermute(f_north, 'lat', north)  3.25 us
    unnamed x19, local copies, waits for them, and re-layouts  2.51 us
  transfers between devices with their start and end apart: 8, of which 3 were waited for; matrix products, arithmetic and copies ran while one was open for 0% of the time, Pallas kernels for 29%

commit v1 on v0

--- a/solution.py
+++ b/solution.py
@@ -11,11 +11,13 @@
 CY = 16
 CX = 256
 BIO_STEP = 0.2
+PRECISE = lax.Precision.HIGHEST
 
 F32 = jnp.float32
 BF16 = jnp.bfloat16
 
 LINES = 14
+PITCH = 65
 BUSY = 10**12
 FR = 26
 NF = NTR * LEV + 1
@@ -53,66 +55,74 @@
     return lax.broadcasted_iota(jnp.int32, (rows, 128), 1)
 
 
-def sort_bands_kernel(bands_ref, tiles_ref, out_ref, xs_ref):
+def sort_bands_kernel(bands_hbm_ref, tiles_hbm_ref, out_ref, xs_ref, ends_ref, tiles_ref, in_sems):
     reader = lax.axis_index("lat") * 16 + lax.axis_index("lon")
-    case = lax.rem(reader, 4)
-    rows = 16
-    for i in range(4):
-
-        @pl.when(case == i)
-        def _(i=i):
-            spare = 0 if i % 2 else 64
-            first = (0, 1, 1, 2)[i]
-            lane = lane_iota(rows)
-            pad = jnp.zeros((rows, 64), F32)
-            for g in range(128 // rows):
-                here = pl.ds(g * rows, rows)
-                x = bands_ref[0, here, :]
-                x = jnp.concatenate([pad, x] if i % 2 else [x, pad], axis=1)
-                xs_ref[here, : LINES * 128] = x
-                ends = jnp.zeros((rows, 128), F32)
-                starts = jnp.zeros((rows, 128), F32)
-                for j in range(7):
-                    line = first + 2 * j
-                    at = spare + 8 * j
-                    if not (i == 3 and j == 6):
-                        moved = x[:, line * 128 : line * 128 + 128]
-                        if at:
-                            moved = pltpu.roll(moved, at, 1)
-                        starts = jnp.where((lane >= at) & (lane < at + 3), moved, starts)
-                    if not (i == 0 and j == 0):
-                        moved = x[:, line * 128 - 128 : line * 128]
-                        if (at + 8) % 128:
-                            moved = pltpu.roll(moved, at + 8, 1)
-                        ends = jnp.where((lane >= at + 5) & (lane < at + 8), moved, ends)
-                xs_ref[here, LINES * 128 : LINES * 128 + 128] = ends
-                xs_ref[here, LINES * 128 + 128 :] = starts
-
+    odd = lax.rem(reader, 2)
+    top = pl.multiple_of(8 + 64 * odd, 8)
+    chunk = 432
+    copies = [
+        pltpu.make_async_copy(
+            bands_hbm_ref.at[0, pl.ds(chunk * k, chunk)],
+            xs_ref.at[pl.ds(pl.multiple_of(top + chunk * k, 8), chunk)],
+            in_sems.at[k],
+        )
+        for k in range(4)
+    ]
+    tiles_copy = pltpu.make_async_copy(tiles_hbm_ref, tiles_ref, in_sems.at[4])
+    tiles_copy.start()
+    for copy in copies:
+        copy.start()
+    spare = pl.multiple_of(64 * (1 - odd), 8)
+    xs_ref[0:8, :] = jnp.zeros((8, 128), F32)
+    xs_ref[8 + LINES * 128 : 16 + LINES * 128, :] = jnp.zeros((8, 128), F32)
+    xs_ref[pl.ds(pl.multiple_of(8 + 27 * 64 * (1 - odd), 8), 64), :] = jnp.zeros((64, 128), F32)
+    ends_ref[...] = jnp.zeros(ends_ref.shape, F32)
+
+    tiles_copy.wait()
     tiles = tiles_ref[0:1, :]
     me = lax.broadcasted_iota(jnp.int32, (128, 128), 0)
     west = (me & -16) | ((me - 1) & 15)
     east = (me & -16) | ((me + 1) & 15)
-    one_hot = [(tiles == t).astype(F32).astype(BF16) for t in (me, west, east)]
-
-    def pick(which, lo, hi):
-        a, b, c = three_parts(xs_ref[:, lo:hi])
-        m = one_hot[which]
-        return (dot(m, c) + dot(m, b)) + dot(m, a)
-
-    base = LINES * 128
-    halo = pick(1, base, base + 128) + pick(2, base + 128, base + 256)
-    odd = lax.rem(reader, 2) == 1
-    for block in range(LINES // 2):
-        t = pick(0, block * 256, block * 256 + 256)
+    own_hot, west_hot, east_hot = [
+        (tiles == t).astype(F32).astype(BF16) for t in (me, west, east)
+    ]
+
+    def pick(hot, k_rows):
+        a, b, c = [
+            lax.dot_general(hot, part, (((1,), (1,)), ((), ())), preferred_element_type=F32)
+            for part in k_rows
+        ]
+        return (c + b) + a
+
+    def sort_block(block, halo):
+        lo = 8 + 256 * block
+        t = pick(own_hot, three_parts(xs_ref[lo : lo + 256, :]))
         for k in range(2):
             line = 2 * block + k
             part = t[:, k * 128 : k * 128 + 128]
             if line == 0:
-                part = part + jnp.where(odd, halo, 0.0)
+                part = part + jnp.where(odd == 1, halo, 0.0)
             if line == LINES - 1:
-                part = part + jnp.where(odd, 0.0, halo)
+                part = part + jnp.where(odd == 1, 0.0, halo)
             for g in range(16):
                 out_ref[pl.ds(8 * LINES * g + line, 8, stride=LINES), :] = part[8 * g : 8 * g + 8]
+
+    arrived = 0
+    for block in range(1, LINES // 2 - 1):
+        while arrived * chunk < 256 * block + 256:
+            copies[arrived].wait()
+            arrived += 1
+        sort_block(block, None)
+    case = lax.rem(reader, 4)
+    first = lax.div(case + 1, 2)
+    for j in range(7):
+        at = 8 + 128 * first + 256 * j
+        ends_ref[pl.ds(spare + 8 * j + 5, 3), :] = xs_ref[pl.ds(at - 3, 3), :]
+        ends_ref[pl.ds(128 + spare + 8 * j, 3), :] = xs_ref[pl.ds(at, 3), :]
+    parts = three_parts(ends_ref[...])
+    halo = pick(west_hot, [p[:128] for p in parts]) + pick(east_hot, [p[128:] for p in parts])
+    sort_block(0, halo)
+    sort_block(LINES // 2 - 1, halo)
 
 
 def north_rows():
@@ -269,13 +279,13 @@
     t_above_ref,
     west_ref,
     east_ref,
-    rates_ref,
+    bio_ref,
     lines_ref,
     below_ref,
     above_ref,
     hot_hbm_ref,
     yrow_ref,
-    out_ref,
+    out_hbm_ref,
     picked_ref,
     flat_ref,
     edge_ref,
@@ -289,14 +299,30 @@
     side1_ref,
     main2_ref,
     side2_ref,
-    coef_ref,
     env_ref,
     lhs_ref,
     hot_ref,
-    hot_sem,
+    rates_ref,
+    out_ref,
+    sems,
+    *work_refs,
 ):
-    hot_copy = pltpu.make_async_copy(hot_hbm_ref, hot_ref, hot_sem)
+    hot_copy = pltpu.make_async_copy(hot_hbm_ref, hot_ref, sems.at[0])
     hot_copy.start()
+
+    shape = (8 * NTR, NTR)
+    spread = lax.broadcasted_iota(jnp.int32, shape, 0) // 8 == lax.broadcasted_iota(jnp.int32, shape, 1)
+    spread = spread.astype(F32)
+    wide = jnp.dot(spread, BIO_STEP * bio_ref[...], preferred_element_type=F32, precision=PRECISE)
+    wide = lax.dot_general(
+        wide, spread, (((1,), (1,)), ((), ())), preferred_element_type=F32, precision=PRECISE
+    )
+    row = lax.broadcasted_iota(jnp.int32, wide.shape, 0)
+    column = lax.broadcasted_iota(jnp.int32, wide.shape, 1)
+    wide = jnp.where((row & 7) == (column & 7), wide, 0.0)
+    hi = wide.astype(BF16)
+    lo = (wide - hi.astype(F32)).astype(BF16)
+    rates_ref[...] = jnp.concatenate([hi, hi, lo], axis=1)
     fill_frames(
         tracers_ref, ocean_ref, t_below_ref, t_above_ref, west_ref, east_ref, below_ref, above_ref,
         main_ref, side_ref, ends_ref,
@@ -321,6 +347,8 @@
                 k = s * LEV + l if f < 2 else s * (LEV + 1) + l + 1
                 for h in range(3):
                     to = (k * 3 + h) * FR
+                    if s == 0:
+                        ref[to + 19 : to + 26, :] = jnp.zeros((7, 128), F32)
                     for g in range(2):
                         if h < 2:
                             part = flat_ref[pl.ds(32 * q + 16 * g + h, 8, stride=2), :]
@@ -343,11 +371,12 @@
         width = 3 if s < 2 else 2
         smain, sside = src
 
-        def body(t, _):
+        def place(t):
             l = lax.div(t, groups)
             g = lax.rem(t, groups)
-            row = start + 8 * g
-
+            return l, g, start + 8 * g
+
+        def readers(row):
             def frame(f, h, off=0):
                 if h < 2:
                     return smain[pl.ds((f * 2 + h) * FR + row + off, 8), :]
@@ -361,6 +390,22 @@
                 if h < 2:
                     return main_ref[pl.ds((f * 2 + h) * FR + row + off, 8), :]
                 return side_ref[pl.ds(f * FR + row + off, 8), :]
+
+            return frame, forcing, ocean
+
+        def prepare(t, slot):
+            split_ref, grown_ref, coef_ref = work_refs[3 * slot : 3 * slot + 3]
+            l, g, row = place(t)
+            frame, forcing, ocean = readers(row)
+            for h in range(width):
+                x = jnp.concatenate([frame(l * NTR + c, h) for c in range(NTR)], axis=0)
+                hi = x.astype(BF16)
+                lo = (x - hi.astype(F32)).astype(BF16)
+                cols = slice(128 * h, 128 * h + 128)
+                split_ref[0:80, cols] = hi
+                split_ref[80:160, cols] = lo
+                split_ref[160:240, cols] = hi
+            grown_ref[:, : 128 * width] = dot(rates_ref[...], split_ref[:, : 128 * width])
 
             o = [ocean(h) for h in range(3)]
             u = [forcing(u_ref, s * LEV + l, h) for h in range(3)]
@@ -382,46 +427,58 @@
                 for i, value in enumerate(values):
                     coef_ref[(h * 8 + i) * 8 : (h * 8 + i) * 8 + 8, :] = value
 
-            def coef(h, i):
-                return coef_ref[(h * 8 + i) * 8 : (h * 8 + i) * 8 + 8, :]
+        def transport(t, slot):
+            grown_ref, coef_ref = work_refs[3 * slot + 1 : 3 * slot + 3]
+            l, g, row = place(t)
+            frame = readers(row)[0]
 
             l_up, l_dn = jnp.minimum(l + 1, LEV - 1), jnp.maximum(l - 1, 0)
-            cells = [[frame(l * NTR + c, h) for h in range(3)] for c in range(NTR)]
+            coefs = [
+                [coef_ref[(h * 8 + i) * 8 : (h * 8 + i) * 8 + 8, :] for i in range(8)]
+                for h in range(width)
+            ]
             for a in range(NTR):
                 f = l * NTR + a
-                rate = rates_ref[a * NTR]
-                grown = [rate * cells[0][h] for h in range(width)]
-                for b in range(1, NTR):
-                    rate = rates_ref[a * NTR + b]
-                    grown = [grown[h] + rate * cells[b][h] for h in range(width)]
-                east, west = shift_east(cells[a], lane), shift_west(cells[a], lane)
+                cell = [frame(f, h) for h in range(3)]
+                east, west = shift_east(cell, lane), shift_west(cell, lane)
                 for h in range(width):
-                    value = coef(h, 0) * cells[a][h] + coef(h, 7) * grown[h]
-                    value = value + coef(h, 1) * east[h] + coef(h, 2) * west[h]
-                    value = value + coef(h, 3) * frame(f, h, 1) + coef(h, 4) * frame(f, h, -1)
-                    value = value + coef(h, 5) * frame(l_up * NTR + a, h)
-                    value = value + coef(h, 6) * frame(l_dn * NTR + a, h)
+                    own, k_e, k_w, k_n, k_s, k_up, k_dn, water = coefs[h]
+                    value = (own * cell[h] + k_e * east[h]) + (k_w * west[h] + k_n * frame(f, h, 1))
+                    value = value + (k_s * frame(f, h, -1) + k_up * frame(l_up * NTR + a, h))
+                    value = value + k_dn * frame(l_dn * NTR + a, h)
+                    value = value + water * grown_ref[8 * a : 8 * a + 8, 128 * h : 128 * h + 128]
                     if s == 2:
                         rows = pl.ds(pl.multiple_of(8 * g, 8), 8)
                         out_ref[a, l, rows, 128 * h : 128 * h + 128] = value
-                        env_ref[h, pl.ds((a * LEV + l) * CY + 8 * g, 8), :] = value
+                        env_ref[h, pl.ds(8 * PITCH * g + a * LEV + l, 8, stride=PITCH), :] = value
                     elif h < 2:
                         dst[0][pl.ds((f * 2 + h) * FR + row, 8), :] = value
                     else:
                         dst[1][pl.ds(f * FR + row, 8), :] = value
+
+        count = groups * LEV
+
+        def body(k, _):
+            prepare(2 * k + 1, 1)
+            transport(2 * k, 0)
+            prepare(jnp.minimum(2 * k + 2, count - 1), 0)
+            transport(2 * k + 1, 1)
             return 0
 
-        lax.fori_loop(0, groups * LEV, body, 0)
+        prepare(0, 0)
+        lax.fori_loop(0, count // 2, body, 0)
 
     substep(0, (main_ref, side_ref), (main1_ref, side1_ref))
     substep(1, (main1_ref, side1_ref), (main2_ref, side2_ref))
     substep(2, (main2_ref, side2_ref), None)
 
-    env_ref[:, NTR * LEV * CY :, :] = jnp.zeros((2, 4 * CY, 128), F32)
+    out_copy = pltpu.make_async_copy(out_ref, out_hbm_ref, sems.at[1])
+    out_copy.start()
+
     for y in range(CY):
         for h in range(2):
-            part = [env_ref[h, pl.ds(128 * k + y, 8, stride=CY), :] for k in range(8)]
-            x = jnp.concatenate(part, axis=0)
+            env_ref[h, PITCH * y + NTR * LEV : PITCH * y + 64, :] = jnp.zeros((4, 128), F32)
+            x = env_ref[h, PITCH * y : PITCH * y + 64, :]
             hi = x.astype(BF16)
             lo = (x - hi.astype(F32)).astype(BF16)
             lhs_ref[128 * y : 128 * y + 64, 128 * h : 128 * h + 128] = hi
@@ -433,13 +490,17 @@
         cols = pl.ds(pl.multiple_of(256 * n, 256), 256)
         found = dot(lhs_ref[...], hot_ref[:, cols])
         row = yrow_ref[0:1, cols]
-        total = jnp.where(row == 0, found[:128], 0.0)
+        total = jnp.where(row == 0, found[:64] + found[64:128], 0.0)
         for y in range(1, CY):
-            total = total + jnp.where(row == y, found[128 * y : 128 * y + 128], 0.0)
-        picked_ref[:, cols] = total.astype(BF16)
+            here = found[128 * y : 128 * y + 64] + found[128 * y + 64 : 128 * y + 128]
+            total = total + jnp.where(row == y, here, 0.0)
+        hi = total.astype(BF16)
+        picked_ref[0:64, cols] = hi
+        picked_ref[64:128, cols] = (total - hi.astype(F32)).astype(BF16)
         return 0
 
     lax.fori_loop(0, 8, slots, 0)
+    out_copy.wait()
 
 
 def slots_kernel(cells_ref, hot_ref, yrow_ref):
@@ -493,11 +554,21 @@
     vmem = pl.BlockSpec(memory_space=pltpu.VMEM)
     hbm = pl.BlockSpec(memory_space=pltpu.HBM)
 
+    bands = jnp.swapaxes(forcing_groups, 1, 2)
     lines = call(
         sort_bands_kernel,
-        full(128 * LINES, 128),
-        [pltpu.VMEM((128, LINES * 128 + 256), F32)],
-    )(forcing_groups, group_tiles)
+        pltpu.VMEM((128 * LINES, 128), F32),
+        [
+            pltpu.VMEM((16 + LINES * 128, 128), F32),
+            pltpu.VMEM((256, 128), F32),
+            pltpu.VMEM((1, 128), jnp.int32),
+            pltpu.SemaphoreType.DMA((5,)),
+        ],
+        in_specs=[hbm, hbm],
+    )(
+        pltpu.with_memory_space_constraint(bands, pltpu.HBM),
+        pltpu.with_memory_space_constraint(group_tiles, pltpu.HBM),
+    )
     lines = lines.reshape(128, 1, LINES * 128)
     lines = lax.all_to_all(lines, ("lat", "lon"), split_axis=0, concat_axis=0, tiled=True)
     lines = lines.reshape(128 * LINES, 128)
@@ -510,12 +581,11 @@
     above = lax.ppermute(to_south, "lat", south)
     from_west = lax.ppermute(to_east, "lon", east)
     from_east = lax.ppermute(to_west, "lon", west)
-    rates = jnp.broadcast_to((BIO_STEP * bio_rates).reshape(NTR * NTR, 1, 1), (NTR * NTR, 8, 128))
     hot, yrow = call(
         slots_kernel, (full(256, 2048, dtype=BF16), full(1, 2048, dtype=jnp.int32))
     )(agent_cells)
-    lines, below, above, from_west, from_east, hot, yrow, rates = lax.optimization_barrier(
-        (lines, below, above, from_west, from_east, hot, yrow, rates)
+    lines, below, above, from_west, from_east, hot, yrow = lax.optimization_barrier(
+        (lines, below, above, from_west, from_east, hot, yrow)
     )
     f_north, f_south = call(
         edge_rows_kernel,
@@ -530,7 +600,7 @@
     n_main, n_side = NTR * LEV * 2 * FR, NTR * LEV * FR
     tracers_out, picked = call(
         transport_kernel,
-        (full(NTR, LEV, CY, CX), full(128, 2048, dtype=BF16)),
+        (pltpu.HBM((NTR, LEV, CY, CX), F32), full(128, 2048, dtype=BF16)),
         [
             pltpu.VMEM((1728, 128), F32),
             pltpu.VMEM((864, 128), F32),
@@ -544,16 +614,24 @@
             pltpu.VMEM((n_side, 128), F32),
             pltpu.VMEM((n_main, 128), F32),
             pltpu.VMEM((n_side, 128), F32),
-            pltpu.VMEM((3 * 8 * 8, 128), F32),
-            pltpu.VMEM((2, 64 * CY, 128), F32),
+            pltpu.VMEM((2, PITCH * CY, 128), F32),
             pltpu.VMEM((128 * CY, 256), BF16),
             pltpu.VMEM((256, 2048), BF16),
-            pltpu.SemaphoreType.DMA,
-        ],
+            pltpu.VMEM((8 * NTR, 24 * NTR), BF16),
+            pltpu.VMEM((NTR, LEV, CY, CX), F32),
+            pltpu.SemaphoreType.DMA((2,)),
+        ]
+        + [
+            pltpu.VMEM((24 * NTR, 384), BF16),
+            pltpu.VMEM((8 * NTR, 384), F32),
+            pltpu.VMEM((3 * 8 * 8, 128), F32),
+        ]
+        * 2,
         limit=20,
         in_specs=[vmem] * 10 + [hbm, vmem],
+        out_specs=(hbm, vmem),
         flops=BUSY,
-    )(tracers, ocean_mask, below, above, from_west, from_east, rates, lines, f_below, f_above, pltpu.with_memory_space_constraint(hot, pltpu.HBM), yrow)
+    )(tracers, ocean_mask, below, above, from_west, from_east, bio_rates, lines, f_below, f_above, pltpu.with_memory_space_constraint(hot, pltpu.HBM), yrow)
 
     agent_state = call(
         agents_kernel,

time: 64.3 us -> 59.7 us (0.928)
  Pallas kernels: 22.9 us -> 20.4 us
  local copies, waits for them, and re-layouts: 2.74 us -> 1.02 us
    pallas_call x2, Pallas kernels: 19.6 us -> 17.1 us  [the longest x1 14 us: shards(): call(transport_kernel, (pltpu.HBM((NTR, LEV, CY, CX), F32), full(128, 204...]
    unnamed x19 -> x16, local copies, waits for them, and re-layouts: 2.51 us -> 1.02 us
  transfers between devices with their start and end apart: 8 -> 8, of which waited for: 3 -> 3; matrix products, arithmetic and copies ran while one was open for 0% -> 0% of each run, Pallas kernels for 29% -> 25%
where the time goes in v1:
time: 59.7 us; the launch traced here: 59.2 us
  starting transfers between devices  31.9 us (53%)
  Pallas kernels  20.4 us (34%)
  waiting for transfers between devices  5.01 us (8%)
  local copies, waits for them, and re-layouts  1.02 us (2%)
  between operations  0.85 us (1%)
    pallas_call x1, Pallas kernels, shards(): call(transport_kernel, (pltpu.HBM((NTR, LEV, CY, CX), F32), full(128, 204...  14 us
    all_to_all x1, starting transfers between devices, shards(): lax.all_to_all(lines, ('lat', 'lon'), split_axis=0, concat_axis=0, tiled=...  11.5 us
    all_to_all x1, starting transfers between devices, shards(): lax.all_to_all(traits, 'lon', split_axis=0, concat_axis=0, tiled=True)  4.25 us
    ppermute x1, starting transfers between devices, shards(): from_east = lax.ppermute(to_west, 'lon', west)  4.14 us
    all_to_all x1, waiting for transfers between devices, shards(): lax.all_to_all(lines, ('lat', 'lon'), split_axis=0, concat_axis=0, tiled=...  3.87 us
    ppermute x1, starting transfers between devices, shards(): below = lax.ppermute(to_north, 'lat', north)  3.54 us
    ppermute x1, starting transfers between devices, shards(): f_below = lax.ppermute(f_north, 'lat', north)  3.25 us
    pallas_call x1, Pallas kernels, shards(): call(sort_bands_kernel, pltpu.VMEM((128 * LINES, 128), F32), [pltpu.VMEM(...  3.12 us
  transfers between devices with their start and end apart: 8, of which 3 were waited for; matrix products, arithmetic and copies ran while one was open for 0% of the time, Pallas kernels for 25%

profile of v1, /device:TPU:1, one launch (start us, length us, event | category | flops | bytes accessed | tf_op | source)
XLA Modules:
  0.0 59.2 jit_solution(82080776629072777)
XLA Ops:
  0.6 3.1 %shard_map.113 = f32[1792,128]{1,0:T(8,128)} custom-call(f32[1,1728,128]{2,1,0:T(8,128)} %bitcast.7, s32[1,128]{1,0:T(1,128)} %tiles_hbm_ref.1), custom_call_target="tpu_custom_call" | custom-call | tf_op jit(solution)/shard_map/pallas_call | solution.py:558
  3.8 0.0 copy-start
  3.8 0.0 copy-start.4
  3.8 11.5 %all-to-all-start = ((f32[128,1,1792]{2,1,0:T(1,128)}), f32[128,1,1792]{2,1,0:T(1,128)S(1)}, u32[]{:S(2)}, u32[]{:S(2)}) async-start(f32[128,1,1792]{2,1,0:T(1,128)} %bitcast.1), calls=%async_computation | async-start | bytes 1835008 | tf_op jit(solution)/shard_map/all_to_all | solution.py:573
  15.3 0.0 copy-start.1
  15.3 0.4 shard_map.114
  15.7 3.5 %collective-permute-start = (f32[366,128]{1,0:T(8,128)S(1)}, f32[366,128]{1,0:T(8,128)S(1)}, u32[]{:S(2)}, u32[]{:S(2)}) collective-permute-start(f32[366,128]{1,0:T(8,128)S(1)} %get-tuple-element.20), channel_id=1, source_target_pairs={{0,16},{16,32},{32,48},{48,64},{64,80},{80,96},{96,112},{1,17},{17... | collective-permute-start | bytes 562184 | tf_op jit(solution)/shard_map/ppermute | solution.py:580
  19.2 1.9 %collective-permute-start.1 = (f32[366,128]{1,0:T(8,128)S(1)}, f32[366,128]{1,0:T(8,128)S(1)}, u32[]{:S(2)}, u32[]{:S(2)}) collective-permute-start(f32[366,128]{1,0:T(8,128)S(1)} %get-tuple-element.21), channel_id=1, source_target_pairs={{16,0},{32,16},{48,32},{64,48},{80,64},{96,80},{112,96},{17,1},{33... | collective-permute-start | bytes 562184 | tf_op jit(solution)/shard_map/ppermute | solution.py:581
  21.2 1.4 %collective-permute-start.2 = (f32[32,128]{1,0:T(8,128)S(1)}, f32[32,128]{1,0:T(8,128)S(1)}, u32[]{:S(2)}, u32[]{:S(2)}) collective-permute-start(f32[32,128]{1,0:T(8,128)S(1)} %get-tuple-element.22), channel_id=1, source_target_pairs={{0,1},{1,2},{2,3},{3,4},{4,5},{5,6},{6,7},{7,8},{8,9},{9,10},{10,1... | collective-permute-start | bytes 49160 | tf_op jit(solution)/shard_map/ppermute | solution.py:582
  22.6 4.1 %collective-permute-start.3 = (f32[32,128]{1,0:T(8,128)S(1)}, f32[32,128]{1,0:T(8,128)S(1)}, u32[]{:S(2)}, u32[]{:S(2)}) collective-permute-start(f32[32,128]{1,0:T(8,128)S(1)} %get-tuple-element.23), channel_id=1, source_target_pairs={{1,0},{2,1},{3,2},{4,3},{5,4},{6,5},{7,6},{8,7},{9,8},{10,9},{11,1... | collective-permute-start | bytes 49160 | tf_op jit(solution)/shard_map/ppermute | solution.py:583
  26.7 0.3 shard_map.115
  27.0 1.0 %copy-done.6 = bf16[256,2048]{1,0:T(8,128)(2,1)} copy-done((bf16[256,2048]{1,0:T(8,128)(2,1)}, bf16[256,2048]{1,0:T(8,128)(2,1)S(1)}, u32[]{:S(2)}) %copy-start.6) | copy-done | bytes 1048600
  28.0 0.9 %collective-permute-done.2.west_ref = f32[32,128]{1,0:T(8,128)S(1)} collective-permute-done((f32[32,128]{1,0:T(8,128)S(1)}, f32[32,128]{1,0:T(8,128)S(1)}, u32[]{:S(2)}, u32[]{:S(2)}) %collective-permute-start.2) | collective-permute-done | bytes 16416 | tf_op jit(solution)/shard_map/ppermute | solution.py:582
  28.9 0.2 collective-permute-done.1.t_above_ref
  29.1 3.9 %all-to-all-done = f32[128,1,1792]{2,1,0:T(1,128)S(1)} async-done(((f32[128,1,1792]{2,1,0:T(1,128)}), f32[128,1,1792]{2,1,0:T(1,128)S(1)}, u32[]{:S(2)}, u32[]{:S(2)}) %all-to-all-start) | async-done | bytes 917536 | tf_op jit(solution)/shard_map/all_to_all | solution.py:573
  33.0 0.3 shard_map.116
  33.3 3.3 %collective-permute-start.4 = (f32[219,128]{1,0:T(8,128)S(1)}, f32[219,128]{1,0:T(8,128)S(1)}, u32[]{:S(2)}, u32[]{:S(2)}) collective-permute-start(f32[219,128]{1,0:T(8,128)S(1)} %get-tuple-element.31), channel_id=1, source_target_pairs={{0,16},{16,32},{32,48},{48,64},{64,80},{80,96},{96,112},{1,17},{17... | collective-permute-start | bytes 336392 | tf_op jit(solution)/shard_map/ppermute | solution.py:595
  36.5 1.9 %collective-permute-start.5 = (f32[165,128]{1,0:T(8,128)S(1)}, f32[165,128]{1,0:T(8,128)S(1)}, u32[]{:S(2)}, u32[]{:S(2)}) collective-permute-start(f32[165,128]{1,0:T(8,128)S(1)} %get-tuple-element.32), channel_id=1, source_target_pairs={{16,0},{32,16},{48,32},{64,48},{80,64},{96,80},{112,96},{17,1},{33... | collective-permute-start | bytes 253448 | tf_op jit(solution)/shard_map/ppermute | solution.py:596
  38.5 0.0 copy-start.7
  38.5 4.3 %all-to-all-start.1 = ((f32[16,64,128]{2,1,0:T(8,128)}), f32[16,64,128]{2,1,0:T(8,128)}, u32[]{:S(2)}, u32[]{:S(2)}) async-start(f32[16,64,128]{2,1,0:T(8,128)} %bitcast.3), calls=%async_computation.1 | async-start | bytes 1048576 | tf_op jit(solution)/shard_map/all_to_all | solution.py:598
  42.8 0.0 copy-start.2
  42.8 0.0 copy-start.5
  42.8 14.0 %shard_map.117 = (f32[10,6,16,256]{3,2,1,0:T(8,128)}, bf16[128,2048]{1,0:T(8,128)(2,1)S(1)}) custom-call(f32[10,6,16,256]{3,2,1,0:T(8,128)S(1)} %copy-done, s32[16,256]{1,0:T(8,128)S(1)} %copy-done.4, f32[366,128]{1,0:T(8,128)S(1)} %collective-permute-done.t_below_ref, f32[366,128]{1,0:T(8,128)S(1)} %collective-permute-done.1.t_above_ref, ...), custom_call_target="tpu_custom_call" | custom-call | flops 999999995904 | tf_op jit(solution)/shard_map/pallas_call | solution.py:601
  56.8 2.4 %shard_map.118 = f32[16,64,128]{2,1,0:T(8,128)} custom-call(f32[16,64,128]{2,1,0:T(8,128)} %all-to-all-done.1.traits_ref, bf16[128,2048]{1,0:T(8,128)(2,1)S(1)} %get-tuple-element.37.picked_ref, f32[64,64]{1,0:T(8,128)S(1)} %copy-done.2, f32[60,64]{1,0:T(8,128)S(1)} %copy-done.3, s32[1,16,16]{2,1,0:T(8,128)S(1)} %copy-done.5), custom_call_target="tpu_custom_call" | custom-call | tf_op jit(solution)/shard_map/pallas_call | solution.py:636
  (14 shorter events, 0.0 us)
Async XLA Ops:
  3.8 11.5 %copy-start = (f32[10,6,16,256]{3,2,1,0:T(8,128)S(1)}, f32[10,6,16,256]{3,2,1,0:T(8,128)}, u32[]{:S(2)}) copy-start(f32[10,6,16,256]{3,2,1,0:T(8,128)} %tracers_ref.3) | copy-start | bytes 2949124
  3.8 11.5 %copy-start.4 = (s32[16,256]{1,0:T(8,128)S(1)}, s32[16,256]{1,0:T(8,128)}, u32[]{:S(2)}) copy-start(s32[16,256]{1,0:T(8,128)} %ocean_ref.3) | copy-start | bytes 49156
  3.8 29.2 %all-to-all-start = ((f32[128,1,1792]{2,1,0:T(1,128)}), f32[128,1,1792]{2,1,0:T(1,128)S(1)}, u32[]{:S(2)}, u32[]{:S(2)}) async-start(f32[128,1,1792]{2,1,0:T(1,128)} %bitcast.1), calls=%async_computation | async-start | bytes 1835008 | tf_op jit(solution)/shard_map/all_to_all | solution.py:573
  15.3 11.4 %copy-start.1 = (s32[1,16,16,128]{3,2,1,0:T(8,128)S(1)}, s32[1,16,16,128]{3,2,1,0:T(8,128)}, u32[]{:S(2)}) copy-start(s32[1,16,16,128]{3,2,1,0:T(8,128)} %cells_ref.1) | copy-start | bytes 393220
  15.7 13.2 %collective-permute-start = (f32[366,128]{1,0:T(8,128)S(1)}, f32[366,128]{1,0:T(8,128)S(1)}, u32[]{:S(2)}, u32[]{:S(2)}) collective-permute-start(f32[366,128]{1,0:T(8,128)S(1)} %get-tuple-element.20), channel_id=1, source_target_pairs={{0,16},{16,32},{32,48},{48,64},{64,80},{80,96},{96,112},{1,17},{17... | collective-permute-start | bytes 562184 | tf_op jit(solution)/shard_map/ppermute | solution.py:580
  19.2 9.9 %collective-permute-start.1 = (f32[366,128]{1,0:T(8,128)S(1)}, f32[366,128]{1,0:T(8,128)S(1)}, u32[]{:S(2)}, u32[]{:S(2)}) collective-permute-start(f32[366,128]{1,0:T(8,128)S(1)} %get-tuple-element.21), channel_id=1, source_target_pairs={{16,0},{32,16},{48,32},{64,48},{80,64},{96,80},{112,96},{17,1},{33... | collective-permute-start | bytes 562184 | tf_op jit(solution)/shard_map/ppermute | solution.py:581
  21.2 7.7 %collective-permute-start.2 = (f32[32,128]{1,0:T(8,128)S(1)}, f32[32,128]{1,0:T(8,128)S(1)}, u32[]{:S(2)}, u32[]{:S(2)}) collective-permute-start(f32[32,128]{1,0:T(8,128)S(1)} %get-tuple-element.22), channel_id=1, source_target_pairs={{0,1},{1,2},{2,3},{3,4},{4,5},{5,6},{6,7},{7,8},{8,9},{9,10},{10,1... | collective-permute-start | bytes 49160 | tf_op jit(solution)/shard_map/ppermute | solution.py:582
  22.6 6.3 %collective-permute-start.3 = (f32[32,128]{1,0:T(8,128)S(1)}, f32[32,128]{1,0:T(8,128)S(1)}, u32[]{:S(2)}, u32[]{:S(2)}) collective-permute-start(f32[32,128]{1,0:T(8,128)S(1)} %get-tuple-element.23), channel_id=1, source_target_pairs={{1,0},{2,1},{3,2},{4,3},{5,4},{6,5},{7,6},{8,7},{9,8},{10,9},{11,1... | collective-permute-start | bytes 49160 | tf_op jit(solution)/shard_map/ppermute | solution.py:583
  27.0 1.0 %copy-start.6 = (bf16[256,2048]{1,0:T(8,128)(2,1)}, bf16[256,2048]{1,0:T(8,128)(2,1)S(1)}, u32[]{:S(2)}) copy-start(bf16[256,2048]{1,0:T(8,128)(2,1)S(1)} %get-tuple-element.33.hot_hbm_ref) | copy-start | bytes 3145732
  33.3 9.5 %collective-permute-start.4 = (f32[219,128]{1,0:T(8,128)S(1)}, f32[219,128]{1,0:T(8,128)S(1)}, u32[]{:S(2)}, u32[]{:S(2)}) collective-permute-start(f32[219,128]{1,0:T(8,128)S(1)} %get-tuple-element.31), channel_id=1, source_target_pairs={{0,16},{16,32},{32,48},{48,64},{64,80},{80,96},{96,112},{1,17},{17... | collective-permute-start | bytes 336392 | tf_op jit(solution)/shard_map/ppermute | solution.py:595
  36.5 6.2 %collective-permute-start.5 = (f32[165,128]{1,0:T(8,128)S(1)}, f32[165,128]{1,0:T(8,128)S(1)}, u32[]{:S(2)}, u32[]{:S(2)}) collective-permute-start(f32[165,128]{1,0:T(8,128)S(1)} %get-tuple-element.32), channel_id=1, source_target_pairs={{16,0},{32,16},{48,32},{64,48},{80,64},{96,80},{112,96},{17,1},{33... | collective-permute-start | bytes 253448 | tf_op jit(solution)/shard_map/ppermute | solution.py:596
  38.5 4.3 %copy-start.7 = (f32[10,10]{1,0:T(8,128)S(1)}, f32[10,10]{1,0:T(8,128)}, u32[]{:S(2)}) copy-start(f32[10,10]{1,0:T(8,128)} %bio_ref.1) | copy-start | bytes 1204
  38.5 18.3 %all-to-all-start.1 = ((f32[16,64,128]{2,1,0:T(8,128)}), f32[16,64,128]{2,1,0:T(8,128)}, u32[]{:S(2)}, u32[]{:S(2)}) async-start(f32[16,64,128]{2,1,0:T(8,128)} %bitcast.3), calls=%async_computation.1 | async-start | bytes 1048576 | tf_op jit(solution)/shard_map/all_to_all | solution.py:598
  42.8 14.1 %copy-start.2 = (f32[64,64]{1,0:T(8,128)S(1)}, f32[64,64]{1,0:T(8,128)}, u32[]{:S(2)}) copy-start(f32[64,64]{1,0:T(8,128)} %tw_ref.1) | copy-start | bytes 49156
  42.8 14.1 %copy-start.3 = (f32[60,64]{1,0:T(8,128)S(1)}, f32[60,64]{1,0:T(8,128)}, u32[]{:S(2)}) copy-start(f32[60,64]{1,0:T(8,128)} %ew_ref.1) | copy-start | bytes 46084
  42.8 14.1 %copy-start.5 = (s32[1,16,16]{2,1,0:T(8,128)S(1)}, s32[1,16,16]{2,1,0:T(8,128)}, u32[]{:S(2)}) copy-start(s32[1,16,16]{2,1,0:T(8,128)} %counts_ref.1) | copy-start | bytes 3076

commit v2 on v1

--- a/solution.py
+++ b/solution.py
@@ -512,7 +512,13 @@
         yrow_ref[:, 128 * n : 128 * n + 128] = lax.shift_right_logical(cell, 8)
 
 
-def agents_kernel(traits_ref, picked_ref, tw_ref, ew_ref, counts_ref, out_ref, weights_ref):
+def agents_kernel(
+    traits_ref, picked_ref, tw_ref, ew_ref, counts_ref, out_hbm_ref, out_ref, weights_ref, sems
+):
+    first, second = [
+        pltpu.make_async_copy(out_ref.at[here], out_hbm_ref.at[here], sems.at[k])
+        for k, here in enumerate((pl.ds(0, 8), pl.ds(8, 8)))
+    ]
     own = lax.axis_index("lon")
     ew = jnp.concatenate([ew_ref[...], jnp.zeros((4, 64), F32)], axis=0)
     for k, w in enumerate((tw_ref[...], ew)):
@@ -532,6 +538,11 @@
         for k in range(2):
             live = slot < counts_ref[0, n + k, own]
             out_ref[n + k] = jnp.where(live, new[:, 128 * k : 128 * k + 128], 0.0)
+        if n == 6:
+            first.start()
+    second.start()
+    first.wait()
+    second.wait()
 
 
 def shards(
@@ -635,9 +646,14 @@
 
     agent_state = call(
         agents_kernel,
-        full(16, 64, 128),
-        [pltpu.VMEM((64, 384), BF16)],
+        pltpu.HBM((16, 64, 128), F32),
+        [
+            pltpu.VMEM((16, 64, 128), F32),
+            pltpu.VMEM((64, 384), BF16),
+            pltpu.SemaphoreType.DMA((2,)),
+        ],
         in_specs=[vmem] * 4 + [pl.BlockSpec(memory_space=pltpu.SMEM)],
+        out_specs=hbm,
     )(received, picked, trait_weights, env_weights, agent_counts)
     return (tracers_out, agent_state[None, None])
 

time: 59.7 us -> 59.6 us (level)
  no operation moved by 1% of the time
where the time goes in v2:
time: 59.6 us; the launch traced here: 59.1 us
  starting transfers between devices  31.9 us (54%)
  Pallas kernels  20.3 us (34%)
  waiting for transfers between devices  5.01 us (8%)
  local copies, waits for them, and re-layouts  1.02 us (2%)
  between operations  0.85 us (1%)
    pallas_call x1, Pallas kernels, shards(): call(transport_kernel, (pltpu.HBM((NTR, LEV, CY, CX), F32), full(128, 204...  14 us
    all_to_all x1, starting transfers between devices, shards(): lax.all_to_all(lines, ('lat', 'lon'), split_axis=0, concat_axis=0, tiled=...  11.5 us
    all_to_all x1, starting transfers between devices, shards(): lax.all_to_all(traits, 'lon', split_axis=0, concat_axis=0, tiled=True)  4.25 us
    ppermute x1, starting transfers between devices, shards(): from_east = lax.ppermute(to_west, 'lon', west)  4.14 us
    all_to_all x1, waiting for transfers between devices, shards(): lax.all_to_all(lines, ('lat', 'lon'), split_axis=0, concat_axis=0, tiled=...  3.87 us
    ppermute x1, starting transfers between devices, shards(): below = lax.ppermute(to_north, 'lat', north)  3.54 us
    ppermute x1, starting transfers between devices, shards(): f_below = lax.ppermute(f_north, 'lat', north)  3.25 us
    pallas_call x1, Pallas kernels, shards(): call(sort_bands_kernel, pltpu.VMEM((128 * LINES, 128), F32), [pltpu.VMEM(...  3.12 us
  transfers between devices with their start and end apart: 8, of which 3 were waited for; matrix products, arithmetic and copies ran while one was open for 0% of the time, Pallas kernels for 25%

profile of v2, /device:TPU:1, one launch (start us, length us, event | category | flops | bytes accessed | tf_op | source)
XLA Modules:
  0.0 59.1 jit_solution(15271596542294777552)
XLA Ops:
  0.6 3.1 %shard_map.113 = f32[1792,128]{1,0:T(8,128)} custom-call(f32[1,1728,128]{2,1,0:T(8,128)} %bitcast.7, s32[1,128]{1,0:T(1,128)} %tiles_hbm_ref.1), custom_call_target="tpu_custom_call" | custom-call | tf_op jit(solution)/shard_map/pallas_call | solution.py:569
  3.8 0.0 copy-start
  3.8 0.0 copy-start.4
  3.8 11.5 %all-to-all-start = ((f32[128,1,1792]{2,1,0:T(1,128)}), f32[128,1,1792]{2,1,0:T(1,128)S(1)}, u32[]{:S(2)}, u32[]{:S(2)}) async-start(f32[128,1,1792]{2,1,0:T(1,128)} %bitcast.1), calls=%async_computation | async-start | bytes 1835008 | tf_op jit(solution)/shard_map/all_to_all | solution.py:584
  15.3 0.0 copy-start.1
  15.3 0.4 shard_map.114
  15.7 3.5 %collective-permute-start = (f32[366,128]{1,0:T(8,128)S(1)}, f32[366,128]{1,0:T(8,128)S(1)}, u32[]{:S(2)}, u32[]{:S(2)}) collective-permute-start(f32[366,128]{1,0:T(8,128)S(1)} %get-tuple-element.20), channel_id=1, source_target_pairs={{0,16},{16,32},{32,48},{48,64},{64,80},{80,96},{96,112},{1,17},{17... | collective-permute-start | bytes 562184 | tf_op jit(solution)/shard_map/ppermute | solution.py:591
  19.2 1.9 %collective-permute-start.1 = (f32[366,128]{1,0:T(8,128)S(1)}, f32[366,128]{1,0:T(8,128)S(1)}, u32[]{:S(2)}, u32[]{:S(2)}) collective-permute-start(f32[366,128]{1,0:T(8,128)S(1)} %get-tuple-element.21), channel_id=1, source_target_pairs={{16,0},{32,16},{48,32},{64,48},{80,64},{96,80},{112,96},{17,1},{33... | collective-permute-start | bytes 562184 | tf_op jit(solution)/shard_map/ppermute | solution.py:592
  21.2 1.4 %collective-permute-start.2 = (f32[32,128]{1,0:T(8,128)S(1)}, f32[32,128]{1,0:T(8,128)S(1)}, u32[]{:S(2)}, u32[]{:S(2)}) collective-permute-start(f32[32,128]{1,0:T(8,128)S(1)} %get-tuple-element.22), channel_id=1, source_target_pairs={{0,1},{1,2},{2,3},{3,4},{4,5},{5,6},{6,7},{7,8},{8,9},{9,10},{10,1... | collective-permute-start | bytes 49160 | tf_op jit(solution)/shard_map/ppermute | solution.py:593
  22.6 4.1 %collective-permute-start.3 = (f32[32,128]{1,0:T(8,128)S(1)}, f32[32,128]{1,0:T(8,128)S(1)}, u32[]{:S(2)}, u32[]{:S(2)}) collective-permute-start(f32[32,128]{1,0:T(8,128)S(1)} %get-tuple-element.23), channel_id=1, source_target_pairs={{1,0},{2,1},{3,2},{4,3},{5,4},{6,5},{7,6},{8,7},{9,8},{10,9},{11,1... | collective-permute-start | bytes 49160 | tf_op jit(solution)/shard_map/ppermute | solution.py:594
  26.7 0.3 shard_map.115
  27.0 1.0 %copy-done.6 = bf16[256,2048]{1,0:T(8,128)(2,1)} copy-done((bf16[256,2048]{1,0:T(8,128)(2,1)}, bf16[256,2048]{1,0:T(8,128)(2,1)S(1)}, u32[]{:S(2)}) %copy-start.6) | copy-done | bytes 1048600
  28.0 0.9 %collective-permute-done.2.west_ref = f32[32,128]{1,0:T(8,128)S(1)} collective-permute-done((f32[32,128]{1,0:T(8,128)S(1)}, f32[32,128]{1,0:T(8,128)S(1)}, u32[]{:S(2)}, u32[]{:S(2)}) %collective-permute-start.2) | collective-permute-done | bytes 16416 | tf_op jit(solution)/shard_map/ppermute | solution.py:593
  28.9 0.2 collective-permute-done.1.t_above_ref
  29.1 3.9 %all-to-all-done = f32[128,1,1792]{2,1,0:T(1,128)S(1)} async-done(((f32[128,1,1792]{2,1,0:T(1,128)}), f32[128,1,1792]{2,1,0:T(1,128)S(1)}, u32[]{:S(2)}, u32[]{:S(2)}) %all-to-all-start) | async-done | bytes 917536 | tf_op jit(solution)/shard_map/all_to_all | solution.py:584
  33.0 0.3 shard_map.116
  33.3 3.3 %collective-permute-start.4 = (f32[219,128]{1,0:T(8,128)S(1)}, f32[219,128]{1,0:T(8,128)S(1)}, u32[]{:S(2)}, u32[]{:S(2)}) collective-permute-start(f32[219,128]{1,0:T(8,128)S(1)} %get-tuple-element.31), channel_id=1, source_target_pairs={{0,16},{16,32},{32,48},{48,64},{64,80},{80,96},{96,112},{1,17},{17... | collective-permute-start | bytes 336392 | tf_op jit(solution)/shard_map/ppermute | solution.py:606
  36.5 1.9 %collective-permute-start.5 = (f32[165,128]{1,0:T(8,128)S(1)}, f32[165,128]{1,0:T(8,128)S(1)}, u32[]{:S(2)}, u32[]{:S(2)}) collective-permute-start(f32[165,128]{1,0:T(8,128)S(1)} %get-tuple-element.32), channel_id=1, source_target_pairs={{16,0},{32,16},{48,32},{64,48},{80,64},{96,80},{112,96},{17,1},{33... | collective-permute-start | bytes 253448 | tf_op jit(solution)/shard_map/ppermute | solution.py:607
  38.5 0.0 copy-start.7
  38.5 4.3 %all-to-all-start.1 = ((f32[16,64,128]{2,1,0:T(8,128)}), f32[16,64,128]{2,1,0:T(8,128)}, u32[]{:S(2)}, u32[]{:S(2)}) async-start(f32[16,64,128]{2,1,0:T(8,128)} %bitcast.3), calls=%async_computation.1 | async-start | bytes 1048576 | tf_op jit(solution)/shard_map/all_to_all | solution.py:609
  42.8 0.0 copy-start.2
  42.8 0.0 copy-start.3
  42.8 14.0 %shard_map.117 = (f32[10,6,16,256]{3,2,1,0:T(8,128)}, bf16[128,2048]{1,0:T(8,128)(2,1)S(1)}) custom-call(f32[10,6,16,256]{3,2,1,0:T(8,128)S(1)} %copy-done, s32[16,256]{1,0:T(8,128)S(1)} %copy-done.4, f32[366,128]{1,0:T(8,128)S(1)} %collective-permute-done.t_below_ref, f32[366,128]{1,0:T(8,128)S(1)} %collective-permute-done.1.t_above_ref, ...), custom_call_target="tpu_custom_call" | custom-call | flops 999999995904 | tf_op jit(solution)/shard_map/pallas_call | solution.py:612
  56.8 2.3 %shard_map.118 = f32[16,64,128]{2,1,0:T(8,128)} custom-call(f32[16,64,128]{2,1,0:T(8,128)} %all-to-all-done.1.traits_ref, bf16[128,2048]{1,0:T(8,128)(2,1)S(1)} %get-tuple-element.37.picked_ref, f32[64,64]{1,0:T(8,128)S(1)} %copy-done.2, f32[60,64]{1,0:T(8,128)S(1)} %copy-done.3, s32[1,16,16]{2,1,0:T(8,128)S(1)} %copy-done.5), custom_call_target="tpu_custom_call" | custom-call | tf_op jit(solution)/shard_map/pallas_call | solution.py:647
  (14 shorter events, 0.0 us)
Async XLA Ops:
  3.8 11.5 %copy-start = (f32[10,6,16,256]{3,2,1,0:T(8,128)S(1)}, f32[10,6,16,256]{3,2,1,0:T(8,128)}, u32[]{:S(2)}) copy-start(f32[10,6,16,256]{3,2,1,0:T(8,128)} %tracers_ref.3) | copy-start | bytes 2949124
  3.8 11.5 %copy-start.4 = (s32[16,256]{1,0:T(8,128)S(1)}, s32[16,256]{1,0:T(8,128)}, u32[]{:S(2)}) copy-start(s32[16,256]{1,0:T(8,128)} %ocean_ref.3) | copy-start | bytes 49156
  3.8 29.2 %all-to-all-start = ((f32[128,1,1792]{2,1,0:T(1,128)}), f32[128,1,1792]{2,1,0:T(1,128)S(1)}, u32[]{:S(2)}, u32[]{:S(2)}) async-start(f32[128,1,1792]{2,1,0:T(1,128)} %bitcast.1), calls=%async_computation | async-start | bytes 1835008 | tf_op jit(solution)/shard_map/all_to_all | solution.py:584
  15.3 11.4 %copy-start.1 = (s32[1,16,16,128]{3,2,1,0:T(8,128)S(1)}, s32[1,16,16,128]{3,2,1,0:T(8,128)}, u32[]{:S(2)}) copy-start(s32[1,16,16,128]{3,2,1,0:T(8,128)} %cells_ref.1) | copy-start | bytes 393220
  15.7 13.2 %collective-permute-start = (f32[366,128]{1,0:T(8,128)S(1)}, f32[366,128]{1,0:T(8,128)S(1)}, u32[]{:S(2)}, u32[]{:S(2)}) collective-permute-start(f32[366,128]{1,0:T(8,128)S(1)} %get-tuple-element.20), channel_id=1, source_target_pairs={{0,16},{16,32},{32,48},{48,64},{64,80},{80,96},{96,112},{1,17},{17... | collective-permute-start | bytes 562184 | tf_op jit(solution)/shard_map/ppermute | solution.py:591
  19.2 9.9 %collective-permute-start.1 = (f32[366,128]{1,0:T(8,128)S(1)}, f32[366,128]{1,0:T(8,128)S(1)}, u32[]{:S(2)}, u32[]{:S(2)}) collective-permute-start(f32[366,128]{1,0:T(8,128)S(1)} %get-tuple-element.21), channel_id=1, source_target_pairs={{16,0},{32,16},{48,32},{64,48},{80,64},{96,80},{112,96},{17,1},{33... | collective-permute-start | bytes 562184 | tf_op jit(solution)/shard_map/ppermute | solution.py:592
  21.2 7.7 %collective-permute-start.2 = (f32[32,128]{1,0:T(8,128)S(1)}, f32[32,128]{1,0:T(8,128)S(1)}, u32[]{:S(2)}, u32[]{:S(2)}) collective-permute-start(f32[32,128]{1,0:T(8,128)S(1)} %get-tuple-element.22), channel_id=1, source_target_pairs={{0,1},{1,2},{2,3},{3,4},{4,5},{5,6},{6,7},{7,8},{8,9},{9,10},{10,1... | collective-permute-start | bytes 49160 | tf_op jit(solution)/shard_map/ppermute | solution.py:593
  22.6 6.3 %collective-permute-start.3 = (f32[32,128]{1,0:T(8,128)S(1)}, f32[32,128]{1,0:T(8,128)S(1)}, u32[]{:S(2)}, u32[]{:S(2)}) collective-permute-start(f32[32,128]{1,0:T(8,128)S(1)} %get-tuple-element.23), channel_id=1, source_target_pairs={{1,0},{2,1},{3,2},{4,3},{5,4},{6,5},{7,6},{8,7},{9,8},{10,9},{11,1... | collective-permute-start | bytes 49160 | tf_op jit(solution)/shard_map/ppermute | solution.py:594
  27.0 1.0 %copy-start.6 = (bf16[256,2048]{1,0:T(8,128)(2,1)}, bf16[256,2048]{1,0:T(8,128)(2,1)S(1)}, u32[]{:S(2)}) copy-start(bf16[256,2048]{1,0:T(8,128)(2,1)S(1)} %get-tuple-element.33.hot_hbm_ref) | copy-start | bytes 3145732
  33.3 9.5 %collective-permute-start.4 = (f32[219,128]{1,0:T(8,128)S(1)}, f32[219,128]{1,0:T(8,128)S(1)}, u32[]{:S(2)}, u32[]{:S(2)}) collective-permute-start(f32[219,128]{1,0:T(8,128)S(1)} %get-tuple-element.31), channel_id=1, source_target_pairs={{0,16},{16,32},{32,48},{48,64},{64,80},{80,96},{96,112},{1,17},{17... | collective-permute-start | bytes 336392 | tf_op jit(solution)/shard_map/ppermute | solution.py:606
  36.5 6.2 %collective-permute-start.5 = (f32[165,128]{1,0:T(8,128)S(1)}, f32[165,128]{1,0:T(8,128)S(1)}, u32[]{:S(2)}, u32[]{:S(2)}) collective-permute-start(f32[165,128]{1,0:T(8,128)S(1)} %get-tuple-element.32), channel_id=1, source_target_pairs={{16,0},{32,16},{48,32},{64,48},{80,64},{96,80},{112,96},{17,1},{33... | collective-permute-start | bytes 253448 | tf_op jit(solution)/shard_map/ppermute | solution.py:607
  38.5 4.3 %copy-start.7 = (f32[10,10]{1,0:T(8,128)S(1)}, f32[10,10]{1,0:T(8,128)}, u32[]{:S(2)}) copy-start(f32[10,10]{1,0:T(8,128)} %bio_ref.1) | copy-start | bytes 1204
  38.5 18.3 %all-to-all-start.1 = ((f32[16,64,128]{2,1,0:T(8,128)}), f32[16,64,128]{2,1,0:T(8,128)}, u32[]{:S(2)}, u32[]{:S(2)}) async-start(f32[16,64,128]{2,1,0:T(8,128)} %bitcast.3), calls=%async_computation.1 | async-start | bytes 1048576 | tf_op jit(solution)/shard_map/all_to_all | solution.py:609
  42.8 14.1 %copy-start.2 = (f32[64,64]{1,0:T(8,128)S(1)}, f32[64,64]{1,0:T(8,128)}, u32[]{:S(2)}) copy-start(f32[64,64]{1,0:T(8,128)} %tw_ref.1) | copy-start | bytes 49156
  42.8 14.1 %copy-start.3 = (f32[60,64]{1,0:T(8,128)S(1)}, f32[60,64]{1,0:T(8,128)}, u32[]{:S(2)}) copy-start(f32[60,64]{1,0:T(8,128)} %ew_ref.1) | copy-start | bytes 46084
  42.8 14.1 %copy-start.5 = (s32[1,16,16]{2,1,0:T(8,128)S(1)}, s32[1,16,16]{2,1,0:T(8,128)}, u32[]{:S(2)}) copy-start(s32[1,16,16]{2,1,0:T(8,128)} %counts_ref.1) | copy-start | bytes 3076
